TPU v7x, 32 devices: a whole 2x2x4 slice. The times are simulated.
32 devices in a mesh: groups: 2 (over y), filt: 4 (over z), sp: 2 (over x), in: 2 (over core).
Axes of the slice: x: 2, y: 2, z: 4, core: 2. Of those that a mesh axis runs over, the one named last changes fastest.
Arguments:
- image: bfloat16 [16, 256, 1024], P(('groups', 'sp', 'filt'), None, 'in'), parts along dimension 0, may hold values from -6 to 6
- weight: bfloat16 [3, 3, 1024, 1024], P(None, None, 'filt'), may hold values from -0.0625 to 0.0625
- bias: float32 [1024], P('filt'), may hold values from -3 to 3
- cotangent: bfloat16 [16, 1024, 256], P(('groups', 'sp'), 'filt'), parts along dimension 0, may hold values from -0.029907227 to 0.029907227
Outputs:
- output: bfloat16 [16, 1024, 256], P(('groups', 'sp', 'filt'), None, 'in'), parts along dimension 0
- grad_weight: float32 [6, 3, 1024, 1024], P('groups', None, 'filt', 'in'), parts along dimension 0
- grad_bias: float32 [2048], P(('groups', 'filt')), parts along dimension 0
There are 2 independent parts, one for each index of `groups`. A program takes and returns all parts, laid end to end along the dimension named above; an argument that names none is the same for every part. Nothing has to cross between parts.
All inputs are finite; a program needn't handle non-finite values.
Results may differ from a plain program's by a relative error of at most 0.0055.
Values may be sent and summed in bfloat16 or wider, within the bound.
No kernel may reach another device: no remote copies, remote signals or barrier semaphores. Data moves between devices by JAX's collectives and lax.ppermute only.
A program may use at most 64 MiB of HBM per device.

v0:
```python
import jax
import jax.numpy as jnp
from jax import lax
from jax.sharding import PartitionSpec as P


def with_halo(array, sides, width):
    for axis, dim in sides:
        size, length = (lax.axis_size(axis), array.shape[dim])
        up = [(i, (i + 1) % size) for i in range(size - 1)]
        down = [(j, i) for i, j in up]
        last = lax.slice_in_dim(array, length - width, length, axis=dim)
        initial = lax.slice_in_dim(array, 0, width, axis=dim)
        before = lax.ppermute(last, axis, up)
        after = lax.ppermute(initial, axis, down)
        array = jnp.concatenate([before, array, after], axis=dim)
    return array


def tap_products(padded, weight, row_count, col_count):
    running = jnp.zeros((row_count, weight.shape[2], col_count), jnp.float32)
    for row_tap in range(3):
        for col_tap in range(3):
            window = padded[row_tap : row_tap + row_count, col_tap : col_tap + col_count]
            running = running + jnp.einsum(
                "rwc,dc->rdw", window, weight[row_tap, col_tap], preferred_element_type=jnp.float32
            )
    return running


def tap_gradients(padded, grad_out, row_count, col_count):
    pieces = []
    for row_tap in range(3):
        for col_tap in range(3):
            window = padded[row_tap : row_tap + row_count, col_tap : col_tap + col_count]
            pieces.append(
                jnp.einsum("rwc,rdw->dc", window, grad_out, preferred_element_type=jnp.float32)
            )
    stacked = jnp.stack(pieces)
    return stacked.reshape(3, 3, stacked.shape[1], stacked.shape[2])


def silu_parts(shifted, cotangent):
    sigmoid_v = jax.nn.sigmoid(shifted)
    slope = sigmoid_v * (1.0 + shifted * (1.0 - sigmoid_v))
    grad_out = (cotangent.astype(jnp.float32) * slope).astype(jnp.bfloat16)
    return (sigmoid_v, grad_out)


def on_device(image, weight, bias, cotangent):
    row_count = cotangent.shape[0]
    full_cols = cotangent.shape[2]
    in_count = lax.axis_size("in")
    half_cols = full_cols // in_count
    channels = weight.shape[3]
    own_channels = channels // in_count
    bias_col = bias[None, :, None]
    panel = lax.all_gather(image, "filt", axis=0, tiled=True)
    bordered = with_halo(panel, (("sp", 0),), 1)
    padded = jnp.pad(bordered, ((0, 0), (1, 1), (0, 0)))
    own_weight = lax.dynamic_slice_in_dim(
        weight, lax.axis_index("in") * own_channels, own_channels, 3
    )
    partial_value = tap_products(padded, own_weight, row_count, full_cols)
    shifted = lax.psum(partial_value, "in") + bias_col
    sigmoid_v, grad_out = silu_parts(shifted, cotangent)
    local_weight = tap_gradients(padded, grad_out, row_count, full_cols)
    local_bias = jnp.sum(grad_out.astype(jnp.float32), axis=(0, 2))
    grad_weight, grad_bias = lax.psum((local_weight, local_bias), "sp")
    first_col = lax.axis_index("in") * half_cols
    own_shift = lax.dynamic_slice_in_dim(shifted, first_col, half_cols, 2)
    own_sigmoid = lax.dynamic_slice_in_dim(sigmoid_v, first_col, half_cols, 2)
    activated = own_shift * own_sigmoid
    output = lax.all_to_all(
        activated.astype(jnp.bfloat16), "filt", split_axis=0, concat_axis=1, tiled=True
    )
    return (output, grad_weight, grad_bias)


def solution(mesh):
    placed = (
        P(("groups", "sp", "filt"), None, "in"),
        P(None, None, "filt", None),
        P("filt"),
        P(("groups", "sp"), "filt", None),
    )
    return jax.shard_map(
        on_device,
        mesh=mesh,
        in_specs=placed,
        out_specs=(
            P(("groups", "sp", "filt"), None, "in"),
            P("groups", None, "filt", "in"),
            P(("groups", "filt")),
        ),
        check_vma=False,
    )
```

profile of v0, /device:TPU:0, one launch (start us, length us, event | category | flops | bytes accessed | tf_op | source)
XLA Modules:
  0.0 229.4 jit_solution(2796276300759234209)
XLA Ops:
  7.2 0.0 all-gather.2.cloned.1.call-start
  7.2 0.7 all-gather.2.cloned.1.call-update
  7.9 0.0 all-reduce.4.cloned.1.call-start
  7.9 32.3 %all-gather.2.cloned.1.call-done = bf16[4,256,512]{2,1,0:T(8,128)(2,1)} async-done(((bf16[1,256,512]{2,1,0:T(8,128)(2,1)}), bf16[4,256,512]{2,1,0:T(8,128)(2,1)}) %all-gather.2.cloned.1.call-update) | async-done | bytes 1048592 | tf_op jit(solution)/shard_map/all_gather | solution.py:58
  40.2 1.1 fusion.54
  41.3 3.4 %collective-permute-start = (bf16[1,256,512]{2,1,0:T(8,128)(2,1)S(1)}, bf16[1,256,512]{2,1,0:T(8,128)(2,1)S(1)}, u32[]{:S(2)}, u32[]{:S(2)}) collective-permute-start(bf16[1,256,512]{2,1,0:T(8,128)(2,1)S(1)} %get-tuple-element.6), channel_id=1, source_target_pairs={{0,2},{1,3},{4,6},{5,7},{8,10},{9,11},{12,14},{13,15},{16,18},{17,... | collective-permute-start | bytes 786440 | tf_op jit(solution)/shard_map/ppermute | solution.py:14
  44.7 1.3 collective-permute-start.1
  46.0 1.8 fusion.40
  47.8 2.3 %collective-permute-done = bf16[1,256,512]{2,1,0:T(8,128)(2,1)S(1)} collective-permute-done((bf16[1,256,512]{2,1,0:T(8,128)(2,1)S(1)}, bf16[1,256,512]{2,1,0:T(8,128)(2,1)S(1)}, u32[]{:S(2)}, u32[]{:S(2)}) %collective-permute-start) | collective-permute-done | bytes 262176 | tf_op jit(solution)/shard_map/ppermute | solution.py:14
  50.1 4.1 %collective-permute-done.1 = bf16[1,256,512]{2,1,0:T(8,128)(2,1)S(1)} collective-permute-done((bf16[1,256,512]{2,1,0:T(8,128)(2,1)S(1)}, bf16[1,256,512]{2,1,0:T(8,128)(2,1)S(1)}, u32[]{:S(2)}, u32[]{:S(2)}) %collective-permute-start.1) | collective-permute-done | bytes 262176 | tf_op jit(solution)/shard_map/ppermute | solution.py:15
  54.2 1.6 fusion.5
  55.8 0.0 copy-start
  55.8 1.5 fusion.31
  57.4 1.4 fusion.26
  58.8 1.4 fusion.34
  60.2 1.4 fusion.23
  61.7 0.0 copy-done
  61.7 1.4 fusion.38
  63.1 1.5 fusion.12
  64.6 0.0 copy-start.3
  64.6 1.4 fusion.39
  66.0 2.5 %fusion.9 = f32[4,256,256]{2,1,0:T(8,128)} fusion(f32[256,4,256]{2,0,1:T(8,128)S(1)} %fusion.23, f32[256,4,256]{2,0,1:T(8,128)S(1)} %fusion.39, f32[256,4,256]{2,0,1:T(8,128)S(1)} %fusion.26, f32[256,4,256]{2,0,1:T(8,128)S(1)} %fusion.12, bf16[6,258,512]{2,1,0:T(8,128)(2,1)S(1)} %fusion.5, bf16[3,3,256,1024]{3,2,1,0:T(8,128)(2,1)} %param.5, s32[]{:T(128)S(6)} %add.78, ...), kind=kOutput, calls=%fused_computation.12 | convolution fusion | flops 269484032 | bytes 6553612 | tf_op jit(solution)/shard_map/rwc,dc->rdw/dot_general | solution.py:25
  68.5 0.0 all-reduce.4.cloned.1.call-update
  68.6 0.0 all-reduce.6.cloned.1.call-start
  68.6 18.6 %all-reduce.4.cloned.1.call-done = f32[4,256,256]{2,1,0:T(8,128)} async-done(((f32[4,256,256]{2,1,0:T(8,128)}), f32[4,256,256]{2,1,0:T(8,128)}) %all-reduce.4.cloned.1.call-update) | async-done | bytes 1048592 | tf_op jit(solution)/shard_map/psum | solution.py:65
  87.2 0.0 copy-done.3
  87.2 3.0 %convert_reduce_fusion = (f32[256]{0:T(256)S(1)}, bf16[4,256,256]{2,1,0:T(8,128)(2,1)S(1)}, f32[4,256,256]{2,1,0:T(8,128)}) fusion(bf16[4,256,256]{2,1,0:T(8,128)(2,1)} %param.7, f32[4,256,256]{2,1,0:T(8,128)} %all-reduce.4.cloned.1.call-done, f32[256]{0:T(256)S(1)} %copy-done.3), kind=kLoop, calls=%fused_computation.37 | loop fusion | flops 3407616 | bytes 3147776 | tf_op jit(solution)/shard_map/reduce_sum | solution.py:68
  90.2 0.4 fusion.21
  90.6 0.4 fusion.20
  91.1 0.5 fusion.19
  91.5 0.4 fusion.18
  92.0 0.4 fusion.17
  92.4 0.5 fusion.16
  92.9 0.4 fusion.15
  93.3 0.4 fusion.14
  93.8 0.0 copy-start.1
  93.8 0.5 fusion.13
  94.3 0.0 copy-start.2
  94.3 2.2 copy-done.2
  96.5 0.0 all-reduce.6.cloned.1.call-update
  96.5 0.0 copy-done.1
  96.5 0.3 add_divide_fusion
  96.8 0.8 multiply_convert_fusion.1
  97.6 4.9 %all-to-all-start = ((bf16[4,256,128]{2,1,0:T(8,128)(2,1)}), bf16[4,256,128]{2,1,0:T(8,128)(2,1)S(1)}, u32[]{:S(2)}, u32[]{:S(2)}) async-start(bf16[4,256,128]{2,1,0:T(8,128)(2,1)} %multiply_convert_fusion.1), calls=%async_computation | async-start | bytes 524288 | tf_op jit(solution)/shard_map/all_to_all | solution.py:74
  102.5 5.5 %psum.23 = f32[256]{0:T(256)} all-reduce(f32[256]{0:T(256)S(1)} %get-tuple-element.3), channel_id=1, replica_groups=mesh['groups'=2,'filt'=4,'sp'=2,'in'=2] {'sp'}, use_global_device_ids=true, to_apply=%region_3.4 | all-reduce | flops 256 | bytes 2048 | tf_op jit(solution)/shard_map/psum | solution.py:69
  108.0 3.8 %all-to-all-done = bf16[4,256,128]{2,1,0:T(8,128)(2,1)S(1)} async-done(((bf16[4,256,128]{2,1,0:T(8,128)(2,1)}), bf16[4,256,128]{2,1,0:T(8,128)(2,1)S(1)}, u32[]{:S(2)}, u32[]{:S(2)}) %all-to-all-start) | async-done | bytes 262176 | tf_op jit(solution)/shard_map/all_to_all | solution.py:74
  111.8 105.3 %all-reduce.6.cloned.1.call-done = f32[3,3,256,512]{3,2,1,0:T(8,128)} async-done(((f32[3,3,256,512]{3,2,1,0:T(8,128)}), f32[3,3,256,512]{3,2,1,0:T(8,128)}) %all-reduce.6.cloned.1.call-update) | async-done | bytes 4718608 | tf_op jit(solution)/shard_map/psum | solution.py:69
  217.1 0.7 copy.18
  217.8 5.0 %copy.19 = f32[3,3,256,512]{3,2,1,0:T(8,128)} copy(f32[3,3,256,512]{3,2,1,0:T(8,128)} %all-reduce.6.cloned.1.call-done) | data formatting | bytes 9437184
Async XLA Ops:
  7.2 33.1 %all-gather.2.cloned.1.call-start = ((), (), s32[]{:S(2)}) async-start(), calls=%async_computation.1 | async-start | bytes 1310720 | tf_op jit(solution)/shard_map/all_gather | solution.py:58
  7.9 79.3 %all-reduce.4.cloned.1.call-start = ((), (), s32[]{:S(2)}) async-start(), calls=%async_computation.2 | async-start | bytes 2097152 | tf_op jit(solution)/shard_map/psum | solution.py:65
  41.3 8.8 %collective-permute-start = (bf16[1,256,512]{2,1,0:T(8,128)(2,1)S(1)}, bf16[1,256,512]{2,1,0:T(8,128)(2,1)S(1)}, u32[]{:S(2)}, u32[]{:S(2)}) collective-permute-start(bf16[1,256,512]{2,1,0:T(8,128)(2,1)S(1)} %get-tuple-element.6), channel_id=1, source_target_pairs={{0,2},{1,3},{4,6},{5,7},{8,10},{9,11},{12,14},{13,15},{16,18},{17,... | collective-permute-start | bytes 786440 | tf_op jit(solution)/shard_map/ppermute | solution.py:14
  44.7 9.5 %collective-permute-start.1 = (bf16[1,256,512]{2,1,0:T(8,128)(2,1)S(1)}, bf16[1,256,512]{2,1,0:T(8,128)(2,1)S(1)}, u32[]{:S(2)}, u32[]{:S(2)}) collective-permute-start(bf16[1,256,512]{2,1,0:T(8,128)(2,1)S(1)} %get-tuple-element.7), channel_id=1, source_target_pairs={{2,0},{3,1},{6,4},{7,5},{10,8},{11,9},{14,12},{15,13},{18,16},{19,... | collective-permute-start | bytes 786440 | tf_op jit(solution)/shard_map/ppermute | solution.py:15
  55.8 5.9 %copy-start = (bf16[4,256,512]{2,1,0:T(8,128)(2,1)S(1)}, bf16[4,256,512]{2,1,0:T(8,128)(2,1)}, u32[]{:S(2)}) copy-start(bf16[4,256,512]{2,1,0:T(8,128)(2,1)} %all-gather.2.cloned.1.call-done) | copy-start | bytes 3145732
  64.6 22.6 %copy-start.3 = (f32[256]{0:T(256)S(1)}, f32[256]{0:T(256)}, u32[]{:S(2)}) copy-start(f32[256]{0:T(256)} %param.6) | copy-start | bytes 3076
  68.6 148.6 %all-reduce.6.cloned.1.call-start = ((), (), s32[]{:S(2)}) async-start(), calls=%async_computation.3 | async-start | bytes 9437184 | tf_op jit(solution)/shard_map/psum | solution.py:69
  93.8 2.7 %copy-start.1 = (f32[4,256,256]{2,1,0:T(8,128)S(1)}, f32[4,256,256]{2,1,0:T(8,128)}, u32[]{:S(2)}) copy-start(f32[4,256,256]{2,1,0:T(8,128)} %get-tuple-element.5) | copy-start | bytes 3145732
  94.3 2.2 copy-start.2
  97.6 14.2 %all-to-all-start = ((bf16[4,256,128]{2,1,0:T(8,128)(2,1)}), bf16[4,256,128]{2,1,0:T(8,128)(2,1)S(1)}, u32[]{:S(2)}, u32[]{:S(2)}) async-start(bf16[4,256,128]{2,1,0:T(8,128)(2,1)} %multiply_convert_fusion.1), calls=%async_computation | async-start | bytes 524288 | tf_op jit(solution)/shard_map/all_to_all | solution.py:74
Sparse Core Ops, SparseCore 0:
  9.6 30.6 all-gather.1
  68.7 18.4 all-reduce.3
  96.6 120.4 all-reduce.5
where the time goes:
time: 230 us; the launch traced here: 229 us
  waiting for transfers between devices  167 us (73%)
  matrix products  18.4 us (8%)
  between operations  14 us (6%)
  starting transfers between devices  9.67 us (4%)
  local copies, waits for them, and re-layouts  8.99 us (4%)
  other arithmetic  5.65 us (2%)
  blocking collectives  5.53 us (2%)
    psum x1, waiting for transfers between devices, on_device(): grad_weight, grad_bias = lax.psum((local_weight, local_bias), 'sp')  105 us
    all_gather x1, waiting for transfers between devices, on_device(): panel = lax.all_gather(image, 'filt', axis=0, tiled=True)  32.3 us
    psum x1, waiting for transfers between devices, on_device(): shifted = lax.psum(partial_value, 'in') + bias_col  18.6 us
    dot_general x9, matrix products, tap_products(): jnp.einsum('rwc,dc->rdw', window, weight[row_tap, col_tap], preferred_ele...  14.4 us
    unnamed x10, local copies, waits for them, and re-layouts  7.93 us
    psum x1, blocking collectives, on_device(): grad_weight, grad_bias = lax.psum((local_weight, local_bias), 'sp')  5.53 us
    all_to_all x1, starting transfers between devices, on_device(): lax.all_to_all(activated.astype(jnp.bfloat16), 'filt', split_axis=0, conc...  4.87 us
  transfers between devices with their start and end apart: 6, of which 6 were waited for; matrix products, arithmetic and copies ran while one was open for 1% of the time, Pallas kernels for 0%

commit v1 on v0

v1 whole, which is shorter than its diff:
```python
import functools
import math

import jax
import jax.numpy as jnp
from jax import lax
from jax.experimental import pallas as pl
from jax.experimental.pallas import tpu as pltpu
from jax.sharding import PartitionSpec as P

MIB = 1024 * 1024


def params(*arrays):
    held = sum(math.prod(shape) * size for shape, size in arrays)
    return pltpu.CompilerParams(vmem_limit_bytes=max(20 * MIB, held * 5 // 4 + 8 * MIB))


def shifted_ring(axis, shift):
    size = lax.axis_size(axis)
    return [(i, (i + shift) % size) for i in range(size)]


def gather_blocks(image):
    n_filt, n_sp = lax.axis_size("filt"), lax.axis_size("sp")
    blocks = [[None] * n_filt for _ in range(n_sp)]
    blocks[0][0] = image
    for k in range(n_filt):
        if k:
            blocks[0][k] = lax.ppermute(blocks[0][k - 1], "filt", shifted_ring("filt", 1))
        for j in range(1, n_sp):
            if k and k == n_filt - 1:
                blocks[j][k] = lax.ppermute(blocks[j][0], "filt", shifted_ring("filt", -1))
            else:
                blocks[j][k] = lax.ppermute(blocks[j - 1][k], "sp", shifted_ring("sp", 1))
    return blocks


def move_columns(values, by):
    size = values.shape[1]
    column = lax.broadcasted_iota(jnp.int32, values.shape, 1)
    edge = 0 if by == 1 else size - 1
    return jnp.where(column == edge, 0.0, pltpu.roll(values, by % size, 1))


VMEM = pl.BlockSpec(memory_space=pltpu.VMEM)
SMEM = pl.BlockSpec(memory_space=pltpu.SMEM)
ANY = pl.BlockSpec(memory_space=pl.ANY)


def arrange_kernel(place, weight, out, sems):
    depth = out.shape[1] // 3
    own = weight.shape[2]
    copies = [
        pltpu.make_async_copy(
            weight.at[a, b, :, pl.ds(pl.multiple_of(place[1] * depth, depth), depth)],
            out.at[pl.ds(b * own, own), pl.ds(a * depth, depth)],
            sems.at[a * 3 + b],
        )
        for a in range(3)
        for b in range(3)
    ]
    for copy in copies:
        copy.start()
    for copy in copies:
        copy.wait()


def arrange(place, weight, depth):
    own = weight.shape[2]
    shape = (3 * own, 3 * depth)
    return pl.pallas_call(
        arrange_kernel,
        out_shape=jax.ShapeDtypeStruct(shape, weight.dtype),
        in_specs=[SMEM, ANY],
        out_specs=VMEM,
        scratch_shapes=[pltpu.SemaphoreType.DMA((9,))],
        compiler_params=params((shape, 2)),
        cost_estimate=pl.CostEstimate(
            flops=0, bytes_accessed=36 * own * depth, transcendentals=0
        ),
    )(place, weight)


def forward_kernel(n_blocks, n_sp, j, place, taps, *refs):
    blocks, (out, panel) = refs[:n_blocks], refs[n_blocks:]
    side_rows, own, width = out.shape
    rows_dev, _, depth = blocks[0].shape
    side = lax.rem(place[0] + (n_sp - j), n_sp)
    zeros = jnp.zeros((depth, width), panel.dtype)

    @pl.when(side == 0)
    def _():
        panel[pl.ds(0, depth), :] = zeros

    @pl.when(side == n_sp - 1)
    def _():
        panel[pl.ds((side_rows + 1) * depth, depth), :] = zeros

    for index, block in enumerate(blocks):
        for i in range(rows_dev):
            slot = place[2 + index] * rows_dev + i - side * side_rows + 1

            @pl.when((slot >= 0) & (slot < side_rows + 2))
            def _():
                panel[pl.ds(pl.multiple_of(slot * depth, depth), depth), :] = block[i].T

    @pl.loop(0, side_rows)
    def _(r):
        window = panel[pl.ds(pl.multiple_of(r * depth, depth), 3 * depth), :]
        product = jnp.dot(taps[...], window, preferred_element_type=jnp.float32)
        out[r] = (
            product[own : 2 * own]
            + move_columns(product[:own], 1)
            + move_columns(product[2 * own :], -1)
        )


def forward(place, taps, blocks, side_rows, n_sp, j):
    rows_dev, width, depth = blocks[0].shape
    own = taps.shape[0] // 3
    n_blocks = len(blocks)
    panel = ((side_rows + 2) * depth, width)
    out = (side_rows, own, width)
    return pl.pallas_call(
        functools.partial(forward_kernel, n_blocks, n_sp, j),
        out_shape=jax.ShapeDtypeStruct(out, jnp.float32),
        in_specs=[SMEM, VMEM] + [VMEM] * n_blocks,
        out_specs=VMEM,
        scratch_shapes=[pltpu.VMEM(panel, blocks[0].dtype)],
        compiler_params=params(
            (panel, 2), (out, 4), (taps.shape, 2), ((n_blocks * rows_dev, width, depth), 2)
        ),
        cost_estimate=pl.CostEstimate(
            flops=18 * side_rows * own * width * depth,
            bytes_accessed=18 * own * depth + 6 * side_rows * width * depth,
            transcendentals=0,
        ),
    )(place, taps, *blocks)


def silu_parts(shifted, cotangent):
    sigmoid_v = 0.5 * jnp.tanh(0.5 * shifted) + 0.5
    slope = sigmoid_v * (1.0 + shifted * (1.0 - sigmoid_v))
    grad_out = (cotangent.astype(jnp.float32) * slope).astype(jnp.bfloat16)
    return sigmoid_v, grad_out


def silu_kernel(place, mine, theirs, bias, cotangent, grad_out, activated):
    half = activated.shape[2]

    @pl.loop(0, mine.shape[0])
    def _(r):
        shifted = (mine[r] + theirs[r]) + bias[...]
        sigmoid_v, grad_out[r] = silu_parts(shifted, cotangent[r])
        value = (shifted * sigmoid_v).astype(activated.dtype)
        activated[r] = jnp.where(place[1] == 0, value[:, :half], value[:, half:])


def silu(place, mine, theirs, bias, cotangent):
    rows, own, width = mine.shape
    return pl.pallas_call(
        silu_kernel,
        out_shape=(
            jax.ShapeDtypeStruct((rows, own, width), jnp.bfloat16),
            jax.ShapeDtypeStruct((rows, own, width // 2), jnp.bfloat16),
        ),
        in_specs=[SMEM, VMEM, VMEM, VMEM, VMEM],
        out_specs=(VMEM, VMEM),
        compiler_params=params((mine.shape, 13)),
        cost_estimate=pl.CostEstimate(
            flops=10 * rows * own * width,
            bytes_accessed=13 * rows * own * width,
            transcendentals=rows * own * width,
        ),
    )(place, mine, theirs, bias, cotangent)


def gradient_kernel(n_blocks, n_sp, place, bias, own_grad, *refs):
    blocks, refs = refs[:n_blocks], refs[n_blocks:]
    others, refs = refs[: 4 * (n_sp - 1)], refs[4 * (n_sp - 1) :]
    grad_weight, grad_bias, grads, panel, stage, sems = refs
    rows_dev, width, depth = blocks[0].shape
    side_rows, own, _ = own_grad.shape
    all_rows = n_blocks * rows_dev
    half_rows = side_rows // 2

    def keep(grad_out, row):
        wide = grad_out.astype(jnp.float32)
        at = pl.ds(pl.multiple_of(row * width, width), width)
        grads[pl.ds(0, own), at] = move_columns(wide, -1).astype(grads.dtype)
        grads[pl.ds(own, own), at] = grad_out
        grads[pl.ds(2 * own, own), at] = move_columns(wide, 1).astype(grads.dtype)

    zeros = jnp.zeros((width, depth), panel.dtype)
    panel[pl.ds(0, width), :] = zeros
    panel[pl.ds((all_rows + 1) * width, width), :] = zeros
    for index, block in enumerate(blocks):
        for i in range(rows_dev):
            slot = place[2 + index] * rows_dev + i + 1
            panel[pl.ds(pl.multiple_of(slot * width, width), width), :] = block[i]

    @pl.loop(0, side_rows)
    def _(r):
        keep(own_grad[r], place[0] * side_rows + r)

    for j in range(1, n_sp):
        mine, theirs, near, far = others[4 * (j - 1) : 4 * j]
        side = lax.rem(place[0] + (n_sp - j), n_sp)
        for h, cotangent in enumerate((near, far)):
            start = (place[1] if h == 0 else 1 - place[1]) * half_rows

            @pl.loop(0, half_rows)
            def _(r):
                shifted = (mine[start + r] + theirs[start + r]) + bias[...]
                _, grad_out = silu_parts(shifted, cotangent[r])
                keep(grad_out, side * side_rows + start + r)

    ones = jnp.ones((16, grads.shape[1]), grads.dtype)
    sums = lax.dot_general(
        ones,
        grads[pl.ds(own, own), :],
        (((1,), (1,)), ((), ())),
        preferred_element_type=jnp.float32,
    )
    grad_bias[...] = sums[:1]

    def copy_out(a):
        return pltpu.make_async_copy(stage.at[a], grad_weight.at[a], sems.at[a])

    @pl.loop(0, 3)
    def _(a):
        window = panel[pl.ds(pl.multiple_of(a * width, width), all_rows * width), :]
        product = jnp.dot(grads[...], window, preferred_element_type=jnp.float32)
        stage[a] = product.reshape(3, own, depth)
        copy_out(a).start()

    @pl.loop(0, 3)
    def _(a):
        copy_out(a).wait()


def gradient(place, bias, own_grad, blocks, others, n_sp):
    rows_dev, width, depth = blocks[0].shape
    side_rows, own, _ = own_grad.shape
    n_blocks = len(blocks)
    all_rows = n_blocks * rows_dev
    grads = (3 * own, all_rows * width)
    panel = ((all_rows + 2) * width, depth)
    stage = (3, 3, own, depth)
    return pl.pallas_call(
        functools.partial(gradient_kernel, n_blocks, n_sp),
        out_shape=(
            jax.ShapeDtypeStruct(stage, jnp.float32),
            jax.ShapeDtypeStruct((1, own), jnp.float32),
        ),
        in_specs=[SMEM, VMEM, VMEM] + [VMEM] * (n_blocks + len(others)),
        out_specs=(ANY, VMEM),
        scratch_shapes=[
            pltpu.VMEM(grads, jnp.bfloat16),
            pltpu.VMEM(panel, blocks[0].dtype),
            pltpu.VMEM(stage, jnp.float32),
            pltpu.SemaphoreType.DMA((3,)),
        ],
        compiler_params=params(
            (grads, 2), (panel, 2), (stage, 4), (panel, 2), ((all_rows, own, width), 10)
        ),
        cost_estimate=pl.CostEstimate(
            flops=18 * all_rows * own * width * depth,
            bytes_accessed=36 * own * depth + 2 * all_rows * width * depth,
            transcendentals=all_rows * own * width,
        ),
    )(place, bias, own_grad, *blocks, *others)


def on_device(image, weight, bias, cotangent):
    n_filt, n_sp = lax.axis_size("filt"), lax.axis_size("sp")
    filt, sp, half = lax.axis_index("filt"), lax.axis_index("sp"), lax.axis_index("in")
    side_rows = cotangent.shape[0]
    swap = shifted_ring("in", 1)

    near = lax.dynamic_slice_in_dim(cotangent, half * (side_rows // 2), side_rows // 2, 0)
    halves = []
    for j in range(1, n_sp):
        near = lax.ppermute(near, "sp", shifted_ring("sp", 1))
        halves += [near, lax.ppermute(near, "in", swap)]
    blocks = [block for side in gather_blocks(image) for block in side]

    at = [
        lax.rem(sp + (n_sp - j), n_sp) * n_filt + lax.rem(filt + (n_filt - k), n_filt)
        for j in range(n_sp)
        for k in range(n_filt)
    ]
    place = jnp.stack([sp, half] + at).astype(jnp.int32)
    bias_col = bias.reshape(-1, 1)
    taps = arrange(place, weight, image.shape[2])
    place, taps, bias_col, *halves = lax.optimization_barrier(
        (place, taps, bias_col, *halves)
    )

    partial = [forward(place, taps, blocks, side_rows, n_sp, j) for j in range(n_sp)]
    other = [lax.ppermute(value, "in", swap) for value in partial]

    own_grad, activated = silu(place, partial[0], other[0], bias_col, cotangent)
    output = lax.all_to_all(activated, "filt", split_axis=0, concat_axis=1, tiled=True)
    others = []
    for j in range(1, n_sp):
        others += [partial[j], other[j], *halves[2 * j - 2 : 2 * j]]
    grad_weight, grad_bias = gradient(place, bias_col, own_grad, blocks, others, n_sp)
    return (output, grad_weight, grad_bias.reshape(-1))


def solution(mesh):
    placed = (
        P(("groups", "sp", "filt"), None, "in"),
        P(None, None, "filt", None),
        P("filt"),
        P(("groups", "sp"), "filt", None),
    )
    return jax.shard_map(
        on_device,
        mesh=mesh,
        in_specs=placed,
        out_specs=(
            P(("groups", "sp", "filt"), None, "in"),
            P("groups", None, "filt", "in"),
            P(("groups", "filt")),
        ),
        check_vma=False,
    )
```

time: 230 us -> 79.1 us (0.34)
  waiting for transfers between devices: 167 us -> 17.1 us
  Pallas kernels: 0 us -> 24.1 us
  matrix products: 18.4 us -> 0 us
  between operations: 14 us -> 0.8 us
  local copies, waits for them, and re-layouts: 8.99 us -> 22.1 us
  other arithmetic: 5.65 us -> 0 us
  blocking collectives: 5.53 us -> 0 us
  starting transfers between devices: 9.67 us -> 14.3 us
    psum x2 -> x0, waiting for transfers between devices: 124 us -> none  [the longest x1 105 us: on_device(): grad_weight, grad_bias = lax.psum((local_weight, local_bias), 'sp')]
    all_gather x1 -> x0, waiting for transfers between devices: 32.3 us -> none  [on_device(): panel = lax.all_gather(image, 'filt', axis=0, tiled=True)]
    pallas_call x0 -> x5, Pallas kernels: none -> 24.1 us  [the longest x1 11 us: gradient(): pl.pallas_call(functools.partial(gradient_kernel, n_blocks, n_sp), out_sh...]
    dot_general x18 -> x0, matrix products: 18.4 us -> none  [the longest x9 14.4 us: tap_products(): jnp.einsum('rwc,dc->rdw', window, weight[row_tap, col_tap], preferred_ele...]
    unnamed x10 -> x57, local copies, waits for them, and re-layouts: 7.93 us -> 20.9 us
    ppermute x2 -> x11, waiting for transfers between devices: 6.43 us -> 17.1 us  [the longest x3 9.33 us: gather_blocks(): lax.ppermute(blocks[0][k - 1], 'filt', shifted_ring('filt', 1))]
    ppermute x2 -> x11, starting transfers between devices: 4.68 us -> 10.9 us  [the longest x3 3.34 us: gather_blocks(): blocks[j][k] = lax.ppermute(blocks[j - 1][k], 'sp', shifted_ring('sp', 1))]
    psum x1 -> x0, blocking collectives: 5.53 us -> none  [on_device(): grad_weight, grad_bias = lax.psum((local_weight, local_bias), 'sp')]
  transfers between devices with their start and end apart: 6 -> 12, of which waited for: 6 -> 6; matrix products, arithmetic and copies ran while one was open for 1% -> 2% of each run, Pallas kernels for 0% -> 25%
where the time goes in v1:
time: 79.1 us; the launch traced here: 78.3 us
  Pallas kernels  24.1 us (30%)
  local copies, waits for them, and re-layouts  22.1 us (28%)
  waiting for transfers between devices  17.1 us (22%)
  starting transfers between devices  14.3 us (18%)
  between operations  0.8 us (1%)
    unnamed x57, local copies, waits for them, and re-layouts  20.9 us
    pallas_call x1, Pallas kernels, gradient(): pl.pallas_call(functools.partial(gradient_kernel, n_blocks, n_sp), out_sh...  11 us
    pallas_call x2, Pallas kernels, forward(): pl.pallas_call(functools.partial(forward_kernel, n_blocks, n_sp, j), out_...  10.2 us
    ppermute x3, waiting for transfers between devices, gather_blocks(): lax.ppermute(blocks[0][k - 1], 'filt', shifted_ring('filt', 1))  9.33 us
    ppermute x3, waiting for transfers between devices, gather_blocks(): blocks[j][k] = lax.ppermute(blocks[j - 1][k], 'sp', shifted_ring('sp', 1))  3.64 us
    all_to_all x1, starting transfers between devices, on_device(): lax.all_to_all(activated, 'filt', split_axis=0, concat_axis=1, tiled=True)  3.41 us
    ppermute x3, starting transfers between devices, gather_blocks(): blocks[j][k] = lax.ppermute(blocks[j - 1][k], 'sp', shifted_ring('sp', 1))  3.34 us
    ppermute x3, starting transfers between devices, gather_blocks(): lax.ppermute(blocks[0][k - 1], 'filt', shifted_ring('filt', 1))  3.08 us
  transfers between devices with their start and end apart: 12, of which 6 were waited for; matrix products, arithmetic and copies ran while one was open for 2% of the time, Pallas kernels for 25%

profile of v1, /device:TPU:0, one launch (start us, length us, event | category | flops | bytes accessed | tf_op | source)
XLA Modules:
  0.0 78.3 jit_solution(15132416574379006532)
XLA Ops:
  0.6 0.0 copy-start.2
  0.6 3.1 %collective-permute-start.2 = (bf16[1,256,512]{2,1,0:T(8,128)(2,1)}, bf16[1,256,512]{2,1,0:T(8,128)(2,1)S(1)}, u32[]{:S(2)}, u32[]{:S(2)}) collective-permute-start(bf16[1,256,512]{2,1,0:T(8,128)(2,1)} %refs_0_.5), channel_id=1, source_target_pairs={{0,4},{4,8},{8,12},{12,0},{1,5},{5,9},{9,13},{13,1},{2,6},{6,10},{... | collective-permute-start | bytes 786440 | tf_op jit(solution)/shard_map/ppermute | solution.py:30
  3.7 1.0 %constant_dynamic-slice_fusion = bf16[2,256,256]{2,1,0:T(8,128)(2,1)S(1)} fusion(bf16[4,256,256]{2,1,0:T(8,128)(2,1)} %cotangent.1, s32[]{:T(128)S(6)} %select_n.3), kind=kLoop, calls=%fused_computation | loop fusion | bytes 524292 | tf_op jit(solution)/shard_map/dynamic_slice | solution.py:282
  4.7 1.6 %collective-permute-start = (bf16[2,256,256]{2,1,0:T(8,128)(2,1)S(1)}, bf16[2,256,256]{2,1,0:T(8,128)(2,1)S(1)}, u32[]{:S(2)}, u32[]{:S(2)}) collective-permute-start(bf16[2,256,256]{2,1,0:T(8,128)(2,1)S(1)} %constant_dynamic-slice_fusion), channel_id=1, source_target_pairs={{0,2},{2,0},{1,3},{3,1},{4,6},{6,4},{5,7},{7,5},{8,10},{10,8},{9,1... | collective-permute-start | bytes 786440 | tf_op jit(solution)/shard_map/ppermute | solution.py:285
  6.2 0.5 collective-permute-start.5
  6.8 5.5 %collective-permute-done.2.refs_1_ = bf16[1,256,512]{2,1,0:T(8,128)(2,1)S(1)} collective-permute-done((bf16[1,256,512]{2,1,0:T(8,128)(2,1)}, bf16[1,256,512]{2,1,0:T(8,128)(2,1)S(1)}, u32[]{:S(2)}, u32[]{:S(2)}) %collective-permute-start.2) | collective-permute-done | bytes 262176 | tf_op jit(solution)/shard_map/ppermute | solution.py:30
  12.3 0.0 collective-permute-start.3
  12.3 1.7 %collective-permute-done.refs_10_ = bf16[2,256,256]{2,1,0:T(8,128)(2,1)S(1)} collective-permute-done((bf16[2,256,256]{2,1,0:T(8,128)(2,1)S(1)}, bf16[2,256,256]{2,1,0:T(8,128)(2,1)S(1)}, u32[]{:S(2)}, u32[]{:S(2)}) %collective-permute-start) | collective-permute-done | bytes 262176 | tf_op jit(solution)/shard_map/ppermute | solution.py:285
  14.0 0.0 collective-permute-start.1
  14.0 1.5 %collective-permute-start.6 = (bf16[1,256,512]{2,1,0:T(8,128)(2,1)S(1)}, bf16[1,256,512]{2,1,0:T(8,128)(2,1)S(1)}, u32[]{:S(2)}, u32[]{:S(2)}) collective-permute-start(bf16[1,256,512]{2,1,0:T(8,128)(2,1)S(1)} %collective-permute-done.2.refs_1_), channel_id=1, source_target_pairs={{0,2},{2,0},{1,3},{3,1},{4,6},{6,4},{5,7},{7,5},{8,10},{10,8},{9,1... | collective-permute-start | bytes 786440 | tf_op jit(solution)/shard_map/ppermute | solution.py:35
  15.5 3.6 %collective-permute-done.5.refs_4_ = bf16[1,256,512]{2,1,0:T(8,128)(2,1)S(1)} collective-permute-done((bf16[1,256,512]{2,1,0:T(8,128)(2,1)}, bf16[1,256,512]{2,1,0:T(8,128)(2,1)S(1)}, u32[]{:S(2)}, u32[]{:S(2)}) %collective-permute-start.5) | collective-permute-done | bytes 262176 | tf_op jit(solution)/shard_map/ppermute | solution.py:35
  19.1 2.5 %collective-permute-start.8 = (bf16[1,256,512]{2,1,0:T(8,128)(2,1)S(1)}, bf16[1,256,512]{2,1,0:T(8,128)(2,1)S(1)}, u32[]{:S(2)}, u32[]{:S(2)}) collective-permute-start(bf16[1,256,512]{2,1,0:T(8,128)(2,1)S(1)} %collective-permute-done.5.refs_4_), channel_id=1, source_target_pairs={{0,12},{4,0},{8,4},{12,8},{1,13},{5,1},{9,5},{13,9},{2,14},{6,2},{... | collective-permute-start | bytes 786440 | tf_op jit(solution)/shard_map/ppermute | solution.py:33
  21.6 0.1 collective-permute-done.3.refs_2_
  21.7 1.3 %collective-permute-start.7 = (bf16[1,256,512]{2,1,0:T(8,128)(2,1)S(1)}, bf16[1,256,512]{2,1,0:T(8,128)(2,1)S(1)}, u32[]{:S(2)}, u32[]{:S(2)}) collective-permute-start(bf16[1,256,512]{2,1,0:T(8,128)(2,1)S(1)} %collective-permute-done.3.refs_2_), channel_id=1, source_target_pairs={{0,2},{2,0},{1,3},{3,1},{4,6},{6,4},{5,7},{7,5},{8,10},{10,8},{9,1... | collective-permute-start | bytes 786440 | tf_op jit(solution)/shard_map/ppermute | solution.py:35
  23.0 0.0 collective-permute-start.4
  23.0 0.1 stack.43.place
  23.1 2.3 %copy-done = bf16[3,3,256,1024]{3,2,1,0:T(8,128)(2,1)S(1)} copy-done((bf16[3,3,256,1024]{3,2,1,0:T(8,128)(2,1)S(1)}, bf16[3,3,256,1024]{3,2,1,0:T(8,128)(2,1)}, u32[]{:S(2)}) %copy-start) | copy-done | bytes 4718616
  25.5 0.8 %shard_map.67.taps = bf16[768,1536]{1,0:T(8,128)(2,1)S(1)} custom-call(s32[10]{0:T(128)S(1)} %stack.43.place, bf16[3,3,256,1024]{3,2,1,0:T(8,128)(2,1)S(1)} %copy-done), custom_call_target="tpu_custom_call" | custom-call | bytes 4718592 | tf_op jit(solution)/shard_map/pallas_call | solution.py:72
  26.3 0.0 collective-permute-done.1.refs_11_
  26.3 0.0 copy-start.13
  26.3 0.7 copy-done.13
  27.0 2.4 %collective-permute-done.8.refs_7_ = bf16[1,256,512]{2,1,0:T(8,128)(2,1)S(1)} collective-permute-done((bf16[1,256,512]{2,1,0:T(8,128)(2,1)S(1)}, bf16[1,256,512]{2,1,0:T(8,128)(2,1)S(1)}, u32[]{:S(2)}, u32[]{:S(2)}) %collective-permute-start.8) | collective-permute-done | bytes 262176 | tf_op jit(solution)/shard_map/ppermute | solution.py:33
  29.4 0.0 collective-permute-done.6.refs_5_
  29.4 0.0 collective-permute-done.7.refs_6_
  29.4 3.7 %collective-permute-done.4.refs_3_ = bf16[1,256,512]{2,1,0:T(8,128)(2,1)S(1)} collective-permute-done((bf16[1,256,512]{2,1,0:T(8,128)(2,1)S(1)}, bf16[1,256,512]{2,1,0:T(8,128)(2,1)S(1)}, u32[]{:S(2)}, u32[]{:S(2)}) %collective-permute-start.4) | collective-permute-done | bytes 262176 | tf_op jit(solution)/shard_map/ppermute | solution.py:30
  33.1 0.0 copy-done.7
  33.1 0.0 copy-done.10
  33.1 0.0 copy-done.2
  33.1 4.6 %shard_map.68.mine = f32[4,256,256]{2,1,0:T(8,128)S(1)} custom-call(s32[10]{0:T(128)S(1)} %stack.43.place, bf16[768,1536]{1,0:T(8,128)(2,1)S(1)} %shard_map.67.taps, bf16[1,256,512]{2,1,0:T(8,128)(2,1)S(1)} %copy-done.2, bf16[1,256,512]{2,1,0:T(8,128)(2,1)S(1)} %collective-permute-done.2.refs_1_, bf16[1,256,512]{2,1,0:T(8,128)(2,1)S(1)} %collective-permute-done.3.refs_2_, ...), custom_call_target="tpu_custom_call" | custom-call | flops 2415919104 | bytes 5505024 | tf_op jit(solution)/shard_map/pallas_call | solution.py:125
  37.7 0.0 copy-done.5
  37.8 0.0 copy-start.15
  37.8 0.7 copy-done.15
  38.5 0.7 copy-done.18
  39.2 0.7 copy-done.21
  39.9 0.7 copy-done.24
  40.6 0.0 collective-permute-start.9
  40.6 0.0 copy-done.3
  40.6 1.0 %copy-done.8 = bf16[1,256,512]{2,1,0:T(8,128)(2,1)S(1)} copy-done((bf16[1,256,512]{2,1,0:T(8,128)(2,1)S(1)}, bf16[1,256,512]{2,1,0:T(8,128)(2,1)}, u32[]{:S(2)}) %copy-start.8) | copy-done | bytes 262168
  41.6 0.9 %copy-done.11 = bf16[1,256,512]{2,1,0:T(8,128)(2,1)S(1)} copy-done((bf16[1,256,512]{2,1,0:T(8,128)(2,1)S(1)}, bf16[1,256,512]{2,1,0:T(8,128)(2,1)}, u32[]{:S(2)}) %copy-start.11) | copy-done | bytes 262168
  42.5 0.9 %copy-done.16 = bf16[1,256,512]{2,1,0:T(8,128)(2,1)S(1)} copy-done((bf16[1,256,512]{2,1,0:T(8,128)(2,1)S(1)}, bf16[1,256,512]{2,1,0:T(8,128)(2,1)}, u32[]{:S(2)}) %copy-start.16) | copy-done | bytes 262168
  43.5 0.9 %copy-done.19 = bf16[1,256,512]{2,1,0:T(8,128)(2,1)S(1)} copy-done((bf16[1,256,512]{2,1,0:T(8,128)(2,1)S(1)}, bf16[1,256,512]{2,1,0:T(8,128)(2,1)}, u32[]{:S(2)}) %copy-start.19) | copy-done | bytes 262168
  44.4 0.9 %copy-done.22 = bf16[1,256,512]{2,1,0:T(8,128)(2,1)S(1)} copy-done((bf16[1,256,512]{2,1,0:T(8,128)(2,1)S(1)}, bf16[1,256,512]{2,1,0:T(8,128)(2,1)}, u32[]{:S(2)}) %copy-start.22) | copy-done | bytes 262168
  45.4 0.9 %copy-done.25 = bf16[1,256,512]{2,1,0:T(8,128)(2,1)S(1)} copy-done((bf16[1,256,512]{2,1,0:T(8,128)(2,1)S(1)}, bf16[1,256,512]{2,1,0:T(8,128)(2,1)}, u32[]{:S(2)}) %copy-start.25) | copy-done | bytes 262168
  46.3 5.6 %shard_map.70.refs_8_ = f32[4,256,256]{2,1,0:T(8,128)} custom-call(s32[10]{0:T(128)S(1)} %stack.43.place, bf16[768,1536]{1,0:T(8,128)(2,1)S(1)} %shard_map.67.taps, bf16[1,256,512]{2,1,0:T(8,128)(2,1)S(1)} %copy-done.2, bf16[1,256,512]{2,1,0:T(8,128)(2,1)S(1)} %collective-permute-done.2.refs_1_, bf16[1,256,512]{2,1,0:T(8,128)(2,1)S(1)} %copy-done.11, ...), custom_call_target="tpu_custom_call" | custom-call | flops 2415919104 | bytes 5505024 | tf_op jit(solution)/shard_map/pallas_call | solution.py:125
  51.9 0.4 collective-permute-start.10
  52.4 0.0 copy-done.27
  52.4 0.1 copy.7.bias
  52.5 0.0 collective-permute-done.9.theirs
  52.5 2.0 %shard_map.69 = (bf16[4,256,256]{2,1,0:T(8,128)(2,1)S(1)}, bf16[4,256,128]{2,1,0:T(8,128)(2,1)}) custom-call(s32[10]{0:T(128)S(1)} %stack.43.place, f32[4,256,256]{2,1,0:T(8,128)S(1)} %shard_map.68.mine, f32[4,256,256]{2,1,0:T(8,128)S(1)} %collective-permute-done.9.theirs, f32[256,1]{1,0:T(8,128)S(1)} %copy.7.bias, bf16[4,256,256]{2,1,0:T(8,128)(2,1)S(1)} %copy-done.1), custom_call_target="tpu_custom_call" | custom-call | flops 2621440 | bytes 3407872 | tf_op jit(solution)/shard_map/pallas_call | solution.py:162
  54.6 3.4 %all-to-all-start = ((bf16[4,256,128]{2,1,0:T(8,128)(2,1)}), bf16[4,256,128]{2,1,0:T(8,128)(2,1)S(1)}, u32[]{:S(2)}, u32[]{:S(2)}) async-start(bf16[4,256,128]{2,1,0:T(8,128)(2,1)} %get-tuple-element.15), calls=%async_computation | async-start | bytes 524288 | tf_op jit(solution)/shard_map/all_to_all | solution.py:305
  58.0 0.0 collective-permute-done.10.refs_9_
  58.0 0.0 copy-start.4
  58.0 0.9 %copy-done.4 = bf16[1,256,512]{2,1,0:T(8,128)(2,1)S(1)} copy-done((bf16[1,256,512]{2,1,0:T(8,128)(2,1)S(1)}, bf16[1,256,512]{2,1,0:T(8,128)(2,1)}, u32[]{:S(2)}) %copy-start.4) | copy-done | bytes 262168
  59.0 0.9 %copy-done.6 = bf16[2,256,256]{2,1,0:T(8,128)(2,1)S(1)} copy-done((bf16[2,256,256]{2,1,0:T(8,128)(2,1)S(1)}, bf16[2,256,256]{2,1,0:T(8,128)(2,1)}, u32[]{:S(2)}) %copy-start.6) | copy-done | bytes 262168
  59.9 0.9 %copy-done.9 = bf16[1,256,512]{2,1,0:T(8,128)(2,1)S(1)} copy-done((bf16[1,256,512]{2,1,0:T(8,128)(2,1)S(1)}, bf16[1,256,512]{2,1,0:T(8,128)(2,1)}, u32[]{:S(2)}) %copy-start.9) | copy-done | bytes 262168
  60.9 0.9 %copy-done.12 = bf16[1,256,512]{2,1,0:T(8,128)(2,1)S(1)} copy-done((bf16[1,256,512]{2,1,0:T(8,128)(2,1)S(1)}, bf16[1,256,512]{2,1,0:T(8,128)(2,1)}, u32[]{:S(2)}) %copy-start.12) | copy-done | bytes 262168
  61.8 0.9 %copy-done.14 = bf16[2,256,256]{2,1,0:T(8,128)(2,1)S(1)} copy-done((bf16[2,256,256]{2,1,0:T(8,128)(2,1)S(1)}, bf16[2,256,256]{2,1,0:T(8,128)(2,1)}, u32[]{:S(2)}) %copy-start.14) | copy-done | bytes 262168
  62.8 0.9 %copy-done.17 = bf16[1,256,512]{2,1,0:T(8,128)(2,1)S(1)} copy-done((bf16[1,256,512]{2,1,0:T(8,128)(2,1)S(1)}, bf16[1,256,512]{2,1,0:T(8,128)(2,1)}, u32[]{:S(2)}) %copy-start.17) | copy-done | bytes 262168
  63.7 0.9 %copy-done.20 = bf16[1,256,512]{2,1,0:T(8,128)(2,1)S(1)} copy-done((bf16[1,256,512]{2,1,0:T(8,128)(2,1)S(1)}, bf16[1,256,512]{2,1,0:T(8,128)(2,1)}, u32[]{:S(2)}) %copy-start.20) | copy-done | bytes 262168
  64.7 0.9 %copy-done.23 = bf16[1,256,512]{2,1,0:T(8,128)(2,1)S(1)} copy-done((bf16[1,256,512]{2,1,0:T(8,128)(2,1)S(1)}, bf16[1,256,512]{2,1,0:T(8,128)(2,1)}, u32[]{:S(2)}) %copy-start.23) | copy-done | bytes 262168
  65.6 0.9 %copy-done.26 = bf16[1,256,512]{2,1,0:T(8,128)(2,1)S(1)} copy-done((bf16[1,256,512]{2,1,0:T(8,128)(2,1)S(1)}, bf16[1,256,512]{2,1,0:T(8,128)(2,1)}, u32[]{:S(2)}) %copy-start.26) | copy-done | bytes 262168
  66.6 11.0 %shard_map.71 = (f32[3,3,256,512]{3,2,1,0:T(8,128)}, f32[1,256]{1,0:T(1,128)}) custom-call(s32[10]{0:T(128)S(1)} %stack.43.place, f32[256,1]{1,0:T(8,128)S(1)} %copy.7.bias, bf16[4,256,256]{2,1,0:T(8,128)(2,1)S(1)} %get-tuple-element.16.own_grad, bf16[1,256,512]{2,1,0:T(8,128)(2,1)S(1)} %copy-done.2, bf16[1,256,512]{2,1,0:T(8,128)(2,1)S(1)} %copy-done.4, ...), custom_call_target="tpu_custom_call" | custom-call | flops 4831838208 | bytes 6815744 | tf_op jit(solution)/shard_map/pallas_call | solution.py:251
  77.6 0.0 all-to-all-done
  77.6 0.7 copy.10
  (25 shorter events, 0.0 us)
Async XLA Ops:
  0.6 32.5 %copy-start.2 = (bf16[1,256,512]{2,1,0:T(8,128)(2,1)S(1)}, bf16[1,256,512]{2,1,0:T(8,128)(2,1)}, u32[]{:S(2)}) copy-start(bf16[1,256,512]{2,1,0:T(8,128)(2,1)} %refs_0_.5) | copy-start | bytes 786436
  0.6 11.6 %collective-permute-start.2 = (bf16[1,256,512]{2,1,0:T(8,128)(2,1)}, bf16[1,256,512]{2,1,0:T(8,128)(2,1)S(1)}, u32[]{:S(2)}, u32[]{:S(2)}) collective-permute-start(bf16[1,256,512]{2,1,0:T(8,128)(2,1)} %refs_0_.5), channel_id=1, source_target_pairs={{0,4},{4,8},{8,12},{12,0},{1,5},{5,9},{9,13},{13,1},{2,6},{6,10},{... | collective-permute-start | bytes 786440 | tf_op jit(solution)/shard_map/ppermute | solution.py:30
  4.7 9.3 %collective-permute-start = (bf16[2,256,256]{2,1,0:T(8,128)(2,1)S(1)}, bf16[2,256,256]{2,1,0:T(8,128)(2,1)S(1)}, u32[]{:S(2)}, u32[]{:S(2)}) collective-permute-start(bf16[2,256,256]{2,1,0:T(8,128)(2,1)S(1)} %constant_dynamic-slice_fusion), channel_id=1, source_target_pairs={{0,2},{2,0},{1,3},{3,1},{4,6},{6,4},{5,7},{7,5},{8,10},{10,8},{9,1... | collective-permute-start | bytes 786440 | tf_op jit(solution)/shard_map/ppermute | solution.py:285
  6.2 12.9 %collective-permute-start.5 = (bf16[1,256,512]{2,1,0:T(8,128)(2,1)}, bf16[1,256,512]{2,1,0:T(8,128)(2,1)S(1)}, u32[]{:S(2)}, u32[]{:S(2)}) collective-permute-start(bf16[1,256,512]{2,1,0:T(8,128)(2,1)} %refs_0_.5), channel_id=1, source_target_pairs={{0,2},{2,0},{1,3},{3,1},{4,6},{6,4},{5,7},{7,5},{8,10},{10,8},{9,1... | collective-permute-start | bytes 786440 | tf_op jit(solution)/shard_map/ppermute | solution.py:35
  12.3 28.3 %copy-start.3 = (bf16[1,256,512]{2,1,0:T(8,128)(2,1)}, bf16[1,256,512]{2,1,0:T(8,128)(2,1)S(1)}, u32[]{:S(2)}) copy-start(bf16[1,256,512]{2,1,0:T(8,128)(2,1)S(1)} %collective-permute-done.2.refs_1_) | copy-start | bytes 786436
  12.3 9.5 %collective-permute-start.3 = (bf16[1,256,512]{2,1,0:T(8,128)(2,1)S(1)}, bf16[1,256,512]{2,1,0:T(8,128)(2,1)S(1)}, u32[]{:S(2)}, u32[]{:S(2)}) collective-permute-start(bf16[1,256,512]{2,1,0:T(8,128)(2,1)S(1)} %collective-permute-done.2.refs_1_), channel_id=1, source_target_pairs={{0,4},{4,8},{8,12},{12,0},{1,5},{5,9},{9,13},{13,1},{2,6},{6,10},{... | collective-permute-start | bytes 786440 | tf_op jit(solution)/shard_map/ppermute | solution.py:30
  14.0 23.8 %copy-start.5 = (bf16[2,256,256]{2,1,0:T(8,128)(2,1)}, bf16[2,256,256]{2,1,0:T(8,128)(2,1)S(1)}, u32[]{:S(2)}) copy-start(bf16[2,256,256]{2,1,0:T(8,128)(2,1)S(1)} %collective-permute-done.refs_10_) | copy-start | bytes 786436
  14.0 12.3 %collective-permute-start.1 = (bf16[2,256,256]{2,1,0:T(8,128)(2,1)S(1)}, bf16[2,256,256]{2,1,0:T(8,128)(2,1)S(1)}, u32[]{:S(2)}, u32[]{:S(2)}) collective-permute-start(bf16[2,256,256]{2,1,0:T(8,128)(2,1)S(1)} %collective-permute-done.refs_10_), channel_id=1, source_target_pairs={{0,1},{1,0},{2,3},{3,2},{4,5},{5,4},{6,7},{7,6},{8,9},{9,8},{10,11... | collective-permute-start | bytes 786440 | tf_op jit(solution)/shard_map/ppermute | solution.py:286
  14.0 15.4 %collective-permute-start.6 = (bf16[1,256,512]{2,1,0:T(8,128)(2,1)S(1)}, bf16[1,256,512]{2,1,0:T(8,128)(2,1)S(1)}, u32[]{:S(2)}, u32[]{:S(2)}) collective-permute-start(bf16[1,256,512]{2,1,0:T(8,128)(2,1)S(1)} %collective-permute-done.2.refs_1_), channel_id=1, source_target_pairs={{0,2},{2,0},{1,3},{3,1},{4,6},{6,4},{5,7},{7,5},{8,10},{10,8},{9,1... | collective-permute-start | bytes 786440 | tf_op jit(solution)/shard_map/ppermute | solution.py:35
  19.1 14.0 %copy-start.7 = (bf16[1,256,512]{2,1,0:T(8,128)(2,1)}, bf16[1,256,512]{2,1,0:T(8,128)(2,1)S(1)}, u32[]{:S(2)}) copy-start(bf16[1,256,512]{2,1,0:T(8,128)(2,1)S(1)} %collective-permute-done.5.refs_4_) | copy-start | bytes 786436
  19.1 10.3 %collective-permute-start.8 = (bf16[1,256,512]{2,1,0:T(8,128)(2,1)S(1)}, bf16[1,256,512]{2,1,0:T(8,128)(2,1)S(1)}, u32[]{:S(2)}, u32[]{:S(2)}) collective-permute-start(bf16[1,256,512]{2,1,0:T(8,128)(2,1)S(1)} %collective-permute-done.5.refs_4_), channel_id=1, source_target_pairs={{0,12},{4,0},{8,4},{12,8},{1,13},{5,1},{9,5},{13,9},{2,14},{6,2},{... | collective-permute-start | bytes 786440 | tf_op jit(solution)/shard_map/ppermute | solution.py:33
  21.7 11.4 %copy-start.10 = (bf16[1,256,512]{2,1,0:T(8,128)(2,1)}, bf16[1,256,512]{2,1,0:T(8,128)(2,1)S(1)}, u32[]{:S(2)}) copy-start(bf16[1,256,512]{2,1,0:T(8,128)(2,1)S(1)} %collective-permute-done.3.refs_2_) | copy-start | bytes 786436
  21.7 7.7 %collective-permute-start.7 = (bf16[1,256,512]{2,1,0:T(8,128)(2,1)S(1)}, bf16[1,256,512]{2,1,0:T(8,128)(2,1)S(1)}, u32[]{:S(2)}, u32[]{:S(2)}) collective-permute-start(bf16[1,256,512]{2,1,0:T(8,128)(2,1)S(1)} %collective-permute-done.3.refs_2_), channel_id=1, source_target_pairs={{0,2},{2,0},{1,3},{3,1},{4,6},{6,4},{5,7},{7,5},{8,10},{10,8},{9,1... | collective-permute-start | bytes 786440 | tf_op jit(solution)/shard_map/ppermute | solution.py:35
  23.0 10.1 %collective-permute-start.4 = (bf16[1,256,512]{2,1,0:T(8,128)(2,1)S(1)}, bf16[1,256,512]{2,1,0:T(8,128)(2,1)S(1)}, u32[]{:S(2)}, u32[]{:S(2)}) collective-permute-start(bf16[1,256,512]{2,1,0:T(8,128)(2,1)S(1)} %collective-permute-done.3.refs_2_), channel_id=1, source_target_pairs={{0,4},{4,8},{8,12},{12,0},{1,5},{5,9},{9,13},{13,1},{2,6},{6,10},{... | collective-permute-start | bytes 786440 | tf_op jit(solution)/shard_map/ppermute | solution.py:30
  23.1 2.3 %copy-start = (bf16[3,3,256,1024]{3,2,1,0:T(8,128)(2,1)S(1)}, bf16[3,3,256,1024]{3,2,1,0:T(8,128)(2,1)}, u32[]{:S(2)}) copy-start(bf16[3,3,256,1024]{3,2,1,0:T(8,128)(2,1)} %weight.1) | copy-start | bytes 14155780
  26.3 0.7 copy-start.13
  37.8 0.7 copy-start.15
  38.5 0.7 copy-start.18
  39.2 0.7 copy-start.21
  39.9 0.7 copy-start.24
  40.6 12.0 %copy-start.1 = (bf16[4,256,256]{2,1,0:T(8,128)(2,1)S(1)}, bf16[4,256,256]{2,1,0:T(8,128)(2,1)}, u32[]{:S(2)}) copy-start(bf16[4,256,256]{2,1,0:T(8,128)(2,1)} %cotangent.1) | copy-start | bytes 1572868
  40.6 12.0 %collective-permute-start.9 = (f32[4,256,256]{2,1,0:T(8,128)S(1)}, f32[4,256,256]{2,1,0:T(8,128)S(1)}, u32[]{:S(2)}, u32[]{:S(2)}) collective-permute-start(f32[4,256,256]{2,1,0:T(8,128)S(1)} %shard_map.68.mine), channel_id=1, source_target_pairs={{0,1},{1,0},{2,3},{3,2},{4,5},{5,4},{6,7},{7,6},{8,9},{9,8},{10,11... | collective-permute-start | bytes 3145736 | tf_op jit(solution)/shard_map/ppermute | solution.py:302
  40.6 1.0 %copy-start.8 = (bf16[1,256,512]{2,1,0:T(8,128)(2,1)S(1)}, bf16[1,256,512]{2,1,0:T(8,128)(2,1)}, u32[]{:S(2)}) copy-start(bf16[1,256,512]{2,1,0:T(8,128)(2,1)} %copy-done.7) | copy-start | bytes 786436
  41.6 0.9 %copy-start.11 = (bf16[1,256,512]{2,1,0:T(8,128)(2,1)S(1)}, bf16[1,256,512]{2,1,0:T(8,128)(2,1)}, u32[]{:S(2)}) copy-start(bf16[1,256,512]{2,1,0:T(8,128)(2,1)} %copy-done.10) | copy-start | bytes 786436
  42.5 0.9 %copy-start.16 = (bf16[1,256,512]{2,1,0:T(8,128)(2,1)S(1)}, bf16[1,256,512]{2,1,0:T(8,128)(2,1)}, u32[]{:S(2)}) copy-start(bf16[1,256,512]{2,1,0:T(8,128)(2,1)} %copy-done.15) | copy-start | bytes 786436
  43.5 0.9 %copy-start.19 = (bf16[1,256,512]{2,1,0:T(8,128)(2,1)S(1)}, bf16[1,256,512]{2,1,0:T(8,128)(2,1)}, u32[]{:S(2)}) copy-start(bf16[1,256,512]{2,1,0:T(8,128)(2,1)} %copy-done.18) | copy-start | bytes 786436
  44.4 0.9 %copy-start.22 = (bf16[1,256,512]{2,1,0:T(8,128)(2,1)S(1)}, bf16[1,256,512]{2,1,0:T(8,128)(2,1)}, u32[]{:S(2)}) copy-start(bf16[1,256,512]{2,1,0:T(8,128)(2,1)} %copy-done.21) | copy-start | bytes 786436
  45.4 0.9 %copy-start.25 = (bf16[1,256,512]{2,1,0:T(8,128)(2,1)S(1)}, bf16[1,256,512]{2,1,0:T(8,128)(2,1)}, u32[]{:S(2)}) copy-start(bf16[1,256,512]{2,1,0:T(8,128)(2,1)} %copy-done.24) | copy-start | bytes 786436
  46.3 6.1 %copy-start.27 = (f32[256]{0:T(256)S(1)}, f32[256]{0:T(256)}, u32[]{:S(2)}) copy-start(f32[256]{0:T(256)} %param.6) | copy-start | bytes 3076
  51.9 6.1 %collective-permute-start.10 = (f32[4,256,256]{2,1,0:T(8,128)}, f32[4,256,256]{2,1,0:T(8,128)}, u32[]{:S(2)}, u32[]{:S(2)}) collective-permute-start(f32[4,256,256]{2,1,0:T(8,128)} %shard_map.70.refs_8_), channel_id=1, source_target_pairs={{0,1},{1,0},{2,3},{3,2},{4,5},{5,4},{6,7},{7,6},{8,9},{9,8},{10,11... | collective-permute-start | bytes 3145736 | tf_op jit(solution)/shard_map/ppermute | solution.py:302
  54.6 23.0 %all-to-all-start = ((bf16[4,256,128]{2,1,0:T(8,128)(2,1)}), bf16[4,256,128]{2,1,0:T(8,128)(2,1)S(1)}, u32[]{:S(2)}, u32[]{:S(2)}) async-start(bf16[4,256,128]{2,1,0:T(8,128)(2,1)} %get-tuple-element.15), calls=%async_computation | async-start | bytes 524288 | tf_op jit(solution)/shard_map/all_to_all | solution.py:305
  58.0 1.0 %copy-start.4 = (bf16[1,256,512]{2,1,0:T(8,128)(2,1)S(1)}, bf16[1,256,512]{2,1,0:T(8,128)(2,1)}, u32[]{:S(2)}) copy-start(bf16[1,256,512]{2,1,0:T(8,128)(2,1)} %copy-done.3) | copy-start | bytes 786436
  59.0 0.9 %copy-start.6 = (bf16[2,256,256]{2,1,0:T(8,128)(2,1)S(1)}, bf16[2,256,256]{2,1,0:T(8,128)(2,1)}, u32[]{:S(2)}) copy-start(bf16[2,256,256]{2,1,0:T(8,128)(2,1)} %copy-done.5) | copy-start | bytes 786436
  59.9 0.9 %copy-start.9 = (bf16[1,256,512]{2,1,0:T(8,128)(2,1)S(1)}, bf16[1,256,512]{2,1,0:T(8,128)(2,1)}, u32[]{:S(2)}) copy-start(bf16[1,256,512]{2,1,0:T(8,128)(2,1)} %copy-done.7) | copy-start | bytes 786436
  60.9 0.9 %copy-start.12 = (bf16[1,256,512]{2,1,0:T(8,128)(2,1)S(1)}, bf16[1,256,512]{2,1,0:T(8,128)(2,1)}, u32[]{:S(2)}) copy-start(bf16[1,256,512]{2,1,0:T(8,128)(2,1)} %copy-done.10) | copy-start | bytes 786436
  61.8 0.9 %copy-start.14 = (bf16[2,256,256]{2,1,0:T(8,128)(2,1)S(1)}, bf16[2,256,256]{2,1,0:T(8,128)(2,1)}, u32[]{:S(2)}) copy-start(bf16[2,256,256]{2,1,0:T(8,128)(2,1)} %copy-done.13) | copy-start | bytes 786436
  62.8 0.9 %copy-start.17 = (bf16[1,256,512]{2,1,0:T(8,128)(2,1)S(1)}, bf16[1,256,512]{2,1,0:T(8,128)(2,1)}, u32[]{:S(2)}) copy-start(bf16[1,256,512]{2,1,0:T(8,128)(2,1)} %copy-done.15) | copy-start | bytes 786436
  63.7 0.9 %copy-start.20 = (bf16[1,256,512]{2,1,0:T(8,128)(2,1)S(1)}, bf16[1,256,512]{2,1,0:T(8,128)(2,1)}, u32[]{:S(2)}) copy-start(bf16[1,256,512]{2,1,0:T(8,128)(2,1)} %copy-done.18) | copy-start | bytes 786436
  64.7 0.9 %copy-start.23 = (bf16[1,256,512]{2,1,0:T(8,128)(2,1)S(1)}, bf16[1,256,512]{2,1,0:T(8,128)(2,1)}, u32[]{:S(2)}) copy-start(bf16[1,256,512]{2,1,0:T(8,128)(2,1)} %copy-done.21) | copy-start | bytes 786436
  65.6 0.9 %copy-start.26 = (bf16[1,256,512]{2,1,0:T(8,128)(2,1)S(1)}, bf16[1,256,512]{2,1,0:T(8,128)(2,1)}, u32[]{:S(2)}) copy-start(bf16[1,256,512]{2,1,0:T(8,128)(2,1)} %copy-done.24) | copy-start | bytes 786436
